TPU v7x, 256 devices: a whole 4x4x8 slice. The times are simulated.
256 devices in a mesh: row: 2 (over core), col: 4 (over x), vis: 32 (over z, y).
Axes of the slice: x: 4, y: 4, z: 8, core: 2. Of those that a mesh axis runs over, the one named last changes fastest.
Arguments:
- text_embed: bfloat16 [32, 256, 5120], P('vis', None, 'row'), may hold values from -6 to 6
- image_embed: bfloat16 [32, 64, 5120], P('vis', 'col', 'row'), may hold values from -6 to 6
- slot_source: int32 [32, 256], replicated, may hold values from -1 to 2047, as said below
- segment_ids: int32 [32, 256], P('vis'), may hold values from 0 to 3, never falling along the last dimension, each value on 1 to 128 neighbouring positions
- prefix_lengths: int32 [32, 4], P('vis'), may hold values from 1 to 1024, 2048 in all within a row
- attn_gain: float32 [5120], P('row'), may hold values from 0.1 to 1.9
- qkv_weight: bfloat16 [5120, 3, 5120], P('row', None, 'col'), may hold values from -0.64286954 to 0.64286954
- out_weight: bfloat16 [5120, 5120], P('col', 'row'), may hold values from -0.5 to 0.5
- cache_keys: bfloat16 [32, 4, 1024, 5120], P('vis', None, 'row', 'col'), may hold values from -48 to 48
- cache_values: bfloat16 [32, 4, 1024, 5120], P('vis', None, 'row', 'col'), may hold values from -6 to 6
Outputs:
- hidden: float32 [32, 256, 5120], P('vis', 'col', 'row')
- new_keys: float32 [32, 256, 5120], P('vis', 'row', 'col')
- new_values: float32 [32, 256, 5120], P('vis', 'row', 'col')
- request_rms: float32 [32, 4], P('vis')
Inputs may be any that keep to these rules, and one draw needn't show every extreme that they name: `slot_source`: every global image index appears in exactly one slot; all other slots hold -1. The image tokens of one producing group fill at most 4 slots of any one group, and in every draw some group holds exactly 4 image tokens of every producing group.
All inputs are finite; a program needn't handle non-finite values.
Results may differ from a plain program's by a relative error of at most 0.012.
The roundings to bfloat16 on the way count: a program that leaves them out, or rounds other values in their place, can miss the bound.
Values may be sent and summed in bfloat16 or wider, within the bound.
A program may use at most 192 MiB of HBM per device.

v0:
```python
import jax
import jax.numpy as jnp
from jax import lax
from jax.sharding import PartitionSpec as P

D = 5120
HD = 128
EPSILON = 1e-06


def combined_all(value, axis, join):
    pieces = jax.tree.map(lambda part: lax.all_gather(part, axis), value)
    head = jax.tree.map(lambda part: part[0], pieces)
    tail = jax.tree.map(lambda part: part[1:], pieces)
    running, _ = lax.scan(lambda running, slab: (join(running, slab), None), head, tail)
    return running


def combine_parts(earlier_part, later_part):
    earlier_peak, earlier_sum, earlier_acc = earlier_part
    later_peak, later_sum, later_acc = later_part
    joint_peak = jnp.maximum(earlier_peak, later_peak)
    earlier_factor = jnp.exp(earlier_peak - joint_peak)
    later_factor = jnp.exp(later_peak - joint_peak)
    joint_sum = earlier_sum * earlier_factor + later_sum * later_factor
    joint_acc = earlier_acc * earlier_factor[..., None] + later_acc * later_factor[..., None]
    return (joint_peak, joint_sum, joint_acc)


def attend_block(queries, key_rows, value_rows, allowed):
    scores = jnp.einsum(
        "thd,khd->htk", queries, key_rows, preferred_element_type=jnp.float32
    ) * HD ** (-0.5)
    masked = jnp.where(allowed[None], scores, -1e30)
    peak_score = jnp.max(masked, axis=2)
    weights = jnp.where(allowed[None], jnp.exp(masked - peak_score[..., None]), 0.0)
    weight_sum = jnp.sum(weights, axis=2)
    summed = jnp.einsum(
        "htk,khd->htd", weights.astype(jnp.bfloat16), value_rows, preferred_element_type=jnp.float32
    )
    return (peak_score, weight_sum, summed)


def per_device(
    text_embed,
    image_embed,
    slot_source,
    segment_ids,
    prefix_lengths,
    attn_gain,
    qkv_weight,
    out_weight,
    cache_keys,
    cache_values,
):
    row_count = lax.axis_size("row")
    col_count = lax.axis_size("col")
    vis_count = lax.axis_size("vis")
    row_index = lax.axis_index("row")
    col_index = lax.axis_index("col")
    vis_index = lax.axis_index("vis")
    text_rows = text_embed[0]
    tokens_here = text_rows.shape[0]
    feature_width = text_rows.shape[1]
    sources = lax.dynamic_index_in_dim(slot_source, vis_index, 0, keepdims=False)
    pieces = lax.all_gather(image_embed, ("col", "vis"), axis=0, tiled=True)
    per_piece = pieces.shape[1]
    flat_rows = pieces.reshape(-1, feature_width)
    safe_index = jnp.maximum(sources, 0)
    group_size = per_piece * col_count
    group_of = safe_index // group_size
    within = safe_index % group_size
    located = (within // per_piece * vis_count + group_of) * per_piece + within % per_piece
    picked_rows = jnp.take(flat_rows, located, axis=0)
    filled = jnp.where((sources >= 0)[:, None], picked_rows, text_rows)
    wide_rows = filled.astype(jnp.float32)
    square_part = jnp.sum(wide_rows * wide_rows, axis=1)
    scaled = (wide_rows * attn_gain).astype(jnp.bfloat16)
    projected = jnp.einsum("td,dkh->tkh", scaled, qkv_weight, preferred_element_type=jnp.float32)
    blocks = tokens_here // row_count
    summed_all, square_sums = lax.psum((projected, square_part), "row")
    inv_rms = lax.rsqrt(square_sums / D + EPSILON)
    queries = (summed_all[:, 0] * inv_rms[:, None]).astype(jnp.bfloat16)
    pair_normed = summed_all[:, 1:] * inv_rms[:, None, None]
    pair_exact = lax.dynamic_slice_in_dim(pair_normed, row_index * blocks, blocks, 0)
    pair_mine = pair_exact.astype(jnp.bfloat16)
    head_width = queries.shape[1]
    heads_here = head_width // HD
    segments = segment_ids[0]
    lengths = prefix_lengths[0]
    request_count = lengths.shape[0]
    cache_block = cache_keys.shape[2]
    request_ids = jnp.arange(request_count, dtype=jnp.int32)
    cache_request = jnp.repeat(request_ids, cache_block)
    cache_position = row_index * cache_block + jnp.tile(
        jnp.arange(cache_block, dtype=jnp.int32), request_count
    )
    cache_ok = (cache_request[None, :] == segments[:, None]) & (
        cache_position < lengths[cache_request]
    )[None, :]
    token_ids = jnp.arange(tokens_here, dtype=jnp.int32)
    block_ids = row_index * blocks + jnp.arange(blocks, dtype=jnp.int32)
    block_segments = lax.dynamic_slice_in_dim(segments, row_index * blocks, blocks, 0)
    prompt_ok = (block_segments[None, :] == segments[:, None]) & (
        block_ids[None, :] <= token_ids[:, None]
    )
    allowed = jnp.concatenate([cache_ok, prompt_ok], axis=1)
    key_rows = jnp.concatenate(
        [cache_keys[0].reshape(-1, head_width), pair_mine[:, 0]], axis=0
    ).reshape(-1, heads_here, HD)
    value_rows = jnp.concatenate(
        [cache_values[0].reshape(-1, head_width), pair_mine[:, 1]], axis=0
    ).reshape(-1, heads_here, HD)
    local_parts = attend_block(
        queries.reshape(tokens_here, heads_here, HD), key_rows, value_rows, allowed
    )
    peak_score, weight_sum, summed = combined_all(local_parts, "row", combine_parts)
    attended = (
        (summed / weight_sum[..., None])
        .transpose(1, 0, 2)
        .reshape(tokens_here, head_width)
        .astype(jnp.bfloat16)
    )
    update = jnp.dot(attended, out_weight, preferred_element_type=jnp.float32)
    shares = lax.psum_scatter(update, "col", scatter_dimension=0, tiled=True)
    share_rows = tokens_here // col_count
    residual = lax.dynamic_slice_in_dim(wide_rows, col_index * share_rows, share_rows, 0)
    hidden = residual + shares
    onehot = (segments[None, :] == request_ids[:, None]).astype(jnp.float32)
    totals = jnp.dot(onehot, square_sums, precision=lax.Precision.HIGHEST)
    counts = jnp.sum(onehot, axis=1)
    request_rms = jnp.sqrt(totals / (counts * D))
    return (hidden[None], pair_exact[:, 0][None], pair_exact[:, 1][None], request_rms[None])


def solution(mesh):
    return jax.shard_map(
        per_device,
        mesh=mesh,
        in_specs=(
            P("vis", None, "row"),
            P("vis", "col", "row"),
            P(),
            P("vis", None),
            P("vis", None),
            P("row"),
            P("row", None, "col"),
            P("col", "row"),
            P("vis", None, "row", "col"),
            P("vis", None, "row", "col"),
        ),
        out_specs=(
            P("vis", "col", "row"),
            P("vis", "row", "col"),
            P("vis", "row", "col"),
            P("vis", None),
        ),
        check_vma=False,
    )
```

profile of v0, /device:TPU:1, one launch (start us, length us, event | category | flops | bytes accessed | tf_op | source)
XLA Modules:
  0.0 334.3 jit_solution(8110566947763616634)
XLA Ops:
  10.1 134.3 %all-gather.8.cloned.1.call-done = bf16[128,16,2560]{2,1,0:T(8,128)(2,1)} async-done(((bf16[1,16,2560]{2,1,0:T(8,128)(2,1)}), bf16[128,16,2560]{2,1,0:T(8,128)(2,1)}) %all-gather.8.cloned.1.call-update) | async-done | bytes 10485776 | tf_op jit(solution)/shard_map/all_gather | solution.py:66
  144.5 9.1 %gather_fusion = bf16[256,2560]{1,0:T(8,128)(2,1)} fusion(bf16[2048,2560]{1,0:T(8,128)(2,1)} %bitcast.111, s32[1024]{0:T(1024)S(1)} %pad_clamp_fusion), kind=kCustom, calls=%fused_computation | custom fusion | bytes 2622464 | tf_op jit(solution)/shard_map/jit(_take)/gather | solution.py:74
  153.6 2.4 multiply_reduce_fusion
  156.0 11.2 %fusion.14 = f32[256,3,1280]{2,0,1:T(8,128)} fusion(bf16[2560,3,1280]{2,0,1:T(8,128)(2,1)} %param.16, f32[256,2560]{1,0:T(8,128)S(1)} %get-tuple-element.33, f32[2560]{0:T(1024)S(1)} %copy-done.1), kind=kOutput, calls=%fused_computation.20 | convolution fusion | flops 5034475520 | bytes 26224640 | tf_op jit(solution)/shard_map/td,dkh->tkh/dot_general | solution.py:79
  167.4 11.3 %reshape.366 = bf16[2048,10,128]{2,1,0:T(8,128)(2,1)} reshape(bf16[1,4,512,1280]{3,2,1,0:T(8,128)(2,1)} %param.18) | data formatting | bytes 10485760 | tf_op jit(solution)/shard_map/concatenate | solution.py:108
  178.7 7.5 %copy.43 = bf16[2048,10,128]{2,0,1:T(8,128)(2,1)} copy(bf16[2048,10,128]{2,1,0:T(8,128)(2,1)} %reshape.366) | data formatting | bytes 10485760 | tf_op jit(solution)/shard_map/concatenate | solution.py:108
  186.2 11.3 %reshape.367 = bf16[2048,10,128]{2,1,0:T(8,128)(2,1)} reshape(bf16[1,4,512,1280]{3,2,1,0:T(8,128)(2,1)} %param.19) | data formatting | bytes 10485760 | tf_op jit(solution)/shard_map/concatenate | solution.py:111
  197.5 7.7 %copy.48 = bf16[2048,10,128]{2,0,1:T(8,128)(2,1)} copy(bf16[2048,10,128]{2,1,0:T(8,128)(2,1)} %reshape.367) | data formatting | bytes 10485760 | tf_op jit(solution)/shard_map/concatenate | solution.py:111
  205.8 2.6 compare_select_fusion.1
  209.0 3.4 %psum.15 = f32[256]{0:T(256)S(1)} all-reduce(f32[256]{0:T(256)S(1)} %get-tuple-element.32), channel_id=1, replica_groups=mesh['row'=2,'col'=4,'vis'=32] {'row'}, use_global_device_ids=true, to_apply=%region_2.3 | all-reduce | flops 256 | bytes 2048 | tf_op jit(solution)/shard_map/psum | solution.py:81
  212.5 2.5 slice.70
  215.0 2.8 copy.40
  227.4 14.4 %fusion = (f32[10,256]{1,0:T(8,128)S(1)}, f32[10,256,2176]{2,1,0:T(8,128)}) fusion(pred[256,2176]{1,0:T(8,128)(4,1)S(1)} %pad_add_fusion, bf16[128,10,128]{2,0,1:T(8,128)(2,1)S(1)} %copy.44, bf16[2048,10,128]{2,0,1:T(8,128)(2,1)} %copy.43, f32[256,10,128]{0,2,1:T(8,128)} %bitcast.113, f32[256]{0:T(256)S(1)} %add_rsqrt_fusion), kind=kOutput, calls=%fused_computation.3 | convolution fusion | flops 1454568960 | bytes 29731840 | tf_op jit(solution)/shard_map/thd,khd->htk/dot_general | solution.py:31
  241.8 13.0 %fusion.3 = f32[10,256,128]{2,1,0:T(8,128)} fusion(f32[10,256,2176]{2,1,0:T(8,128)} %get-tuple-element.47, f32[10,256]{1,0:T(8,128)S(1)} %get-tuple-element.46, pred[256,2176]{1,0:T(8,128)(4,1)S(1)} %pad_add_fusion, bf16[128,10,128]{2,0,1:T(8,128)(2,1)S(1)} %copy-done, bf16[2048,10,128]{2,0,1:T(8,128)(2,1)} %copy.48), kind=kOutput, calls=%fused_computation.6 | convolution fusion | flops 1465057280 | bytes 29730816 | tf_op jit(solution)/shard_map/htk,khd->htd/dot_general | solution.py:38
  256.8 11.7 %fusion.1 = f32[10,256]{1,0:T(8,128)S(1)} fusion(f32[10,256,2176]{2,1,0:T(8,128)} %get-tuple-element.47, f32[10,256]{1,0:T(8,128)S(1)} %get-tuple-element.46, pred[256,2176]{1,0:T(8,128)(4,1)S(1)} %pad_add_fusion), kind=kLoop, calls=%fused_computation.4 | loop fusion | flops 27850240 | bytes 22859776 | tf_op jit(solution)/shard_map/reduce_sum | solution.py:37
  268.5 2.1 all-gather.4
  271.2 3.5 %fusion.44 = (f32[10,256,128]{2,1,0:T(8,128)}, f32[10,256,128]{2,1,0:T(8,128)}) fusion(f32[20,256,128]{2,1,0:T(8,128)} %all-gather.10.cloned.1.call-done), kind=kLoop, calls=%fused_computation.97 | loop fusion | bytes 5242880 | tf_op jit(solution)/shard_map/slice | solution.py:13
  274.7 2.8 copy.57
  277.5 2.8 copy.58
  280.3 2.0 divide_convert_fusion
  282.2 6.3 %fusion.47 = f32[256,2560]{1,0:T(8,128)} fusion(bf16[256,1280]{0,1:T(8,128)(2,1)S(1)} %bitcast.112, bf16[1280,2560]{1,0:T(8,128)(2,1)} %param.17), kind=kOutput, calls=%fused_computation.100 | convolution fusion | flops 1677721600 | bytes 9830400 | tf_op jit(solution)/shard_map/dot_general | solution.py:124
  289.3 2.4 slice_bitcast_fusion
  291.7 34.1 %reduce-scatter.2.cloned.1.call-done = f32[64,2560]{1,0:T(8,128)} async-done(((f32[256,2560]{1,0:T(8,128)}), f32[64,2560]{1,0:T(8,128)}) %reduce-scatter.2.cloned.1.call-update) | async-done | bytes 655376 | tf_op jit(solution)/shard_map/reduce_scatter | solution.py:125
  325.8 2.0 add_bitcast_fusion
  (50 shorter events, 17.2 us)
Async XLA Ops:
  7.2 137.3 %all-gather.8.cloned.1.call-start = ((), (), s32[]{:S(2)}) async-start(), calls=%async_computation.1 | async-start | bytes 10567680 | tf_op jit(solution)/shard_map/all_gather | solution.py:66
  7.9 204.6 %all-reduce.2.cloned.1.call-start = ((), (), s32[]{:S(2)}) async-start(), calls=%async_computation.2 | async-start | bytes 7864320 | tf_op jit(solution)/shard_map/psum | solution.py:81
  153.6 2.4 copy-start.1
  167.2 104.0 %all-gather.10.cloned.1.call-start = ((), (), s32[]{:S(2)}) async-start(), calls=%async_computation.4 | async-start | bytes 3932160 | tf_op jit(solution)/shard_map/all_gather | solution.py:12
  197.5 7.7 %copy-start.2 = (s32[1,4]{1,0:T(1,128)S(1)}, s32[1,4]{1,0:T(1,128)}, u32[]{:S(2)}) copy-start(s32[1,4]{1,0:T(1,128)} %param.14) | copy-start | bytes 52
  197.5 10.9 %copy-start.3 = (s32[1,256]{1,0:T(1,128)S(1)}, s32[1,256]{1,0:T(1,128)}, u32[]{:S(2)}) copy-start(s32[1,256]{1,0:T(1,128)} %param.13) | copy-start | bytes 3076
  217.8 1.7 slice-start
  227.4 14.4 %copy-start = (bf16[128,10,128]{2,0,1:T(8,128)(2,1)S(1)}, bf16[128,10,128]{2,0,1:T(8,128)(2,1)}, u32[]{:S(2)}) copy-start(bf16[128,10,128]{2,0,1:T(8,128)(2,1)} %copy.49) | copy-start | bytes 983044
  254.9 70.9 %reduce-scatter.2.cloned.1.call-start = ((), (), s32[]{:S(2)}) async-start(), calls=%async_computation.3 | async-start | bytes 3276800 | tf_op jit(solution)/shard_map/reduce_scatter | solution.py:125
Sparse Core Ops, SparseCore 0:
  11.5 132.9 all-gather.7
  167.4 33.9 all-reduce.1
  255.0 16.1 all-gather.9
  288.6 37.0 reduce-scatter.1
where the time goes:
time: 336 us; the launch traced here: 334 us
  waiting for transfers between devices  170 us (51%)
  local copies, waits for them, and re-layouts  72.7 us (22%)
  matrix products  45.5 us (14%)
  other arithmetic  24.8 us (7%)
  between operations  13.9 us (4%)
  blocking collectives  7.32 us (2%)
    all_gather x1, waiting for transfers between devices, per_device(): pieces = lax.all_gather(image_embed, ('col', 'vis'), axis=0, tiled=True)  134 us
    reduce_scatter x1, waiting for transfers between devices, per_device(): shares = lax.psum_scatter(update, 'col', scatter_dimension=0, tiled=True)  34.1 us
    concatenate x3, local copies, waits for them, and re-layouts, per_device(): jnp.concatenate([cache_values[0].reshape(-1, head_width), pair_mine[:, 1]...  20.8 us
    concatenate x3, local copies, waits for them, and re-layouts, per_device(): jnp.concatenate([cache_keys[0].reshape(-1, head_width), pair_mine[:, 0]],...  20 us
    dot_general x1, matrix products, attend_block(): jnp.einsum('thd,khd->htk', queries, key_rows, preferred_element_type=jnp....  14.4 us
    dot_general x1, matrix products, attend_block(): jnp.einsum('htk,khd->htd', weights.astype(jnp.bfloat16), value_rows, pref...  13 us
    reduce_sum x1, other arithmetic, attend_block(): weight_sum = jnp.sum(weights, axis=2)  11.7 us
    dot_general x1, matrix products, per_device(): jnp.einsum('td,dkh->tkh', scaled, qkv_weight, preferred_element_type=jnp....  11.2 us
  transfers between devices with their start and end apart: 4, of which 3 were waited for; matrix products, arithmetic and copies ran while one was open for 18% of the time, Pallas kernels for 0%

commit v1 on v0

--- a/solution.py
+++ b/solution.py
@@ -63,7 +63,12 @@
     tokens_here = text_rows.shape[0]
     feature_width = text_rows.shape[1]
     sources = lax.dynamic_index_in_dim(slot_source, vis_index, 0, keepdims=False)
-    pieces = lax.all_gather(image_embed, ("col", "vis"), axis=0, tiled=True)
+    pieces = jnp.concatenate(
+        lax.all_to_all(
+            jnp.stack([image_embed] * lax.axis_size(("col", "vis"))), ("col", "vis"), 0, 0
+        ),
+        axis=0,
+    )
     per_piece = pieces.shape[1]
     flat_rows = pieces.reshape(-1, feature_width)
     safe_index = jnp.maximum(sources, 0)

time: 336 us -> 450 us (1.34)
  waiting for transfers between devices: 170 us -> 256 us
  starting transfers between devices: 0.16 us -> 17.1 us
  local copies, waits for them, and re-layouts: 72.7 us -> 79.3 us
    all_to_all x0 -> x1, waiting for transfers between devices: none -> 225 us  [per_device(): lax.all_to_all(jnp.stack([image_embed] * lax.axis_size(('col', 'vis'))),...]
    all_gather x1 -> x0, waiting for transfers between devices: 134 us -> none  [per_device(): pieces = lax.all_gather(image_embed, ('col', 'vis'), axis=0, tiled=True)]
    all_to_all x0 -> x1, starting transfers between devices: none -> 16.8 us  [per_device(): lax.all_to_all(jnp.stack([image_embed] * lax.axis_size(('col', 'vis'))),...]
    another operation x0 -> x1, local copies, waits for them, and re-layouts: none -> 6.02 us  [per_device(): jnp.stack([image_embed] * lax.axis_size(('col', 'vis')))]
  transfers between devices with their start and end apart: 4 -> 4, of which waited for: 3 -> 2; matrix products, arithmetic and copies ran while one was open for 18% -> 13% of each run, Pallas kernels for 0% -> 0%
where the time goes in v1:
time: 450 us; the launch traced here: 448 us
  waiting for transfers between devices  256 us (57%)
  local copies, waits for them, and re-layouts  79.3 us (18%)
  matrix products  45.7 us (10%)
  other arithmetic  25.1 us (6%)
  starting transfers between devices  17.1 us (4%)
  between operations  13.9 us (3%)
  blocking collectives  11 us (2%)
    all_to_all x1, waiting for transfers between devices, per_device(): lax.all_to_all(jnp.stack([image_embed] * lax.axis_size(('col', 'vis'))),...  225 us
    reduce_scatter x1, waiting for transfers between devices, per_device(): shares = lax.psum_scatter(update, 'col', scatter_dimension=0, tiled=True)  30.9 us
    concatenate x3, local copies, waits for them, and re-layouts, per_device(): jnp.concatenate([cache_values[0].reshape(-1, head_width), pair_mine[:, 1]...  21.6 us
    concatenate x3, local copies, waits for them, and re-layouts, per_device(): jnp.concatenate([cache_keys[0].reshape(-1, head_width), pair_mine[:, 0]],...  19.8 us
    all_to_all x1, starting transfers between devices, per_device(): lax.all_to_all(jnp.stack([image_embed] * lax.axis_size(('col', 'vis'))),...  16.8 us
    dot_general x1, matrix products, attend_block(): jnp.einsum('thd,khd->htk', queries, key_rows, preferred_element_type=jnp....  14.5 us
    dot_general x1, matrix products, attend_block(): jnp.einsum('htk,khd->htd', weights.astype(jnp.bfloat16), value_rows, pref...  13 us
    reduce_sum x1, other arithmetic, attend_block(): weight_sum = jnp.sum(weights, axis=2)  12 us
  transfers between devices with their start and end apart: 4, of which 2 were waited for; matrix products, arithmetic and copies ran while one was open for 13% of the time, Pallas kernels for 0%

profile of v1, /device:TPU:1, one launch (start us, length us, event | category | flops | bytes accessed | tf_op | source)
XLA Modules:
  0.0 448.0 jit_solution(15001932974803149367)
XLA Ops:
  7.2 6.0 %stack.2 = bf16[128,1,16,2560]{3,2,1,0:T(8,128)(2,1)} broadcast(bf16[16,2560]{1,0:T(8,128)(2,1)} %bitcast.116), dimensions={2,3} | broadcast | bytes 10567680 | tf_op jit(solution)/shard_map/stack | solution.py:68
  13.2 16.8 %all-to-all-start = ((bf16[128,1,16,2560]{3,2,1,0:T(8,128)(2,1)}), bf16[128,1,16,2560]{3,2,1,0:T(8,128)(2,1)}, u32[]{:S(2)}, u32[]{:S(2)}) async-start(bf16[128,1,16,2560]{3,2,1,0:T(8,128)(2,1)} %stack.2), calls=%async_computation | async-start | bytes 20971520 | tf_op jit(solution)/shard_map/all_to_all | solution.py:67
  32.2 224.9 %all-to-all-done = bf16[128,1,16,2560]{3,2,1,0:T(8,128)(2,1)} async-done(((bf16[128,1,16,2560]{3,2,1,0:T(8,128)(2,1)}), bf16[128,1,16,2560]{3,2,1,0:T(8,128)(2,1)}, u32[]{:S(2)}, u32[]{:S(2)}) %all-to-all-start) | async-done | bytes 10485792 | tf_op jit(solution)/shard_map/all_to_all | solution.py:67
  257.1 9.1 %gather_fusion = bf16[256,2560]{1,0:T(8,128)(2,1)} fusion(bf16[2048,2560]{1,0:T(8,128)(2,1)} %bitcast.3, s32[1024]{0:T(1024)S(1)} %pad_clamp_fusion), kind=kCustom, calls=%fused_computation | custom fusion | bytes 2622464 | tf_op jit(solution)/shard_map/jit(_take)/gather | solution.py:79
  266.3 2.4 multiply_reduce_fusion
  268.7 11.2 %fusion.14 = f32[256,3,1280]{2,0,1:T(8,128)} fusion(bf16[2560,3,1280]{2,0,1:T(8,128)(2,1)} %param.16, f32[256,2560]{1,0:T(8,128)S(1)} %get-tuple-element.33, f32[2560]{0:T(1024)S(1)} %copy-done.1), kind=kOutput, calls=%fused_computation.20 | convolution fusion | flops 5034475520 | bytes 26224640 | tf_op jit(solution)/shard_map/td,dkh->tkh/dot_general | solution.py:84
  280.2 11.3 %reshape.365 = bf16[2048,10,128]{2,1,0:T(8,128)(2,1)} reshape(bf16[1,4,512,1280]{3,2,1,0:T(8,128)(2,1)} %param.18) | data formatting | bytes 10485760 | tf_op jit(solution)/shard_map/concatenate | solution.py:113
  291.5 7.3 %copy.43 = bf16[2048,10,128]{2,0,1:T(8,128)(2,1)} copy(bf16[2048,10,128]{2,1,0:T(8,128)(2,1)} %reshape.365) | data formatting | bytes 10485760 | tf_op jit(solution)/shard_map/concatenate | solution.py:113
  298.8 11.3 %reshape.366 = bf16[2048,10,128]{2,1,0:T(8,128)(2,1)} reshape(bf16[1,4,512,1280]{3,2,1,0:T(8,128)(2,1)} %param.19) | data formatting | bytes 10485760 | tf_op jit(solution)/shard_map/concatenate | solution.py:116
  310.1 8.5 %copy.48 = bf16[2048,10,128]{2,0,1:T(8,128)(2,1)} copy(bf16[2048,10,128]{2,1,0:T(8,128)(2,1)} %reshape.366) | data formatting | bytes 10485760 | tf_op jit(solution)/shard_map/concatenate | solution.py:116
  319.2 2.6 compare_select_fusion.1
  322.4 7.0 %psum.15 = f32[256]{0:T(256)S(1)} all-reduce(f32[256]{0:T(256)S(1)} %get-tuple-element.32), channel_id=1, replica_groups=mesh['row'=2,'col'=4,'vis'=32] {'row'}, use_global_device_ids=true, to_apply=%region_2.3 | all-reduce | flops 256 | bytes 2048 | tf_op jit(solution)/shard_map/psum | solution.py:86
  329.5 2.5 slice.70
  332.0 2.8 copy.40
  344.4 14.5 %fusion = (f32[10,256]{1,0:T(8,128)S(1)}, f32[10,256,2176]{2,1,0:T(8,128)}) fusion(pred[256,2176]{1,0:T(8,128)(4,1)S(1)} %pad_add_fusion, bf16[128,10,128]{2,0,1:T(8,128)(2,1)S(1)} %copy.44, bf16[2048,10,128]{2,0,1:T(8,128)(2,1)} %copy.43, f32[256,10,128]{0,2,1:T(8,128)} %bitcast.113, f32[256]{0:T(256)S(1)} %add_rsqrt_fusion), kind=kOutput, calls=%fused_computation.3 | convolution fusion | flops 1454568960 | bytes 29731840 | tf_op jit(solution)/shard_map/thd,khd->htk/dot_general | solution.py:31
  358.9 13.0 %fusion.3 = f32[10,256,128]{2,1,0:T(8,128)} fusion(f32[10,256,2176]{2,1,0:T(8,128)} %get-tuple-element.47, f32[10,256]{1,0:T(8,128)S(1)} %get-tuple-element.46, pred[256,2176]{1,0:T(8,128)(4,1)S(1)} %pad_add_fusion, bf16[128,10,128]{2,0,1:T(8,128)(2,1)S(1)} %copy-done, bf16[2048,10,128]{2,0,1:T(8,128)(2,1)} %copy.48), kind=kOutput, calls=%fused_computation.6 | convolution fusion | flops 1465057280 | bytes 29730816 | tf_op jit(solution)/shard_map/htk,khd->htd/dot_general | solution.py:38
  373.9 12.0 %fusion.1 = f32[10,256]{1,0:T(8,128)S(1)} fusion(f32[10,256,2176]{2,1,0:T(8,128)} %get-tuple-element.47, f32[10,256]{1,0:T(8,128)S(1)} %get-tuple-element.46, pred[256,2176]{1,0:T(8,128)(4,1)S(1)} %pad_add_fusion), kind=kLoop, calls=%fused_computation.4 | loop fusion | flops 27850240 | bytes 22859776 | tf_op jit(solution)/shard_map/reduce_sum | solution.py:37
  385.9 2.1 all-gather.4
  388.1 3.5 fusion.44
  391.6 2.8 copy.57
  394.4 2.8 copy.58
  399.1 6.3 %fusion.47 = f32[256,2560]{1,0:T(8,128)} fusion(bf16[256,1280]{0,1:T(8,128)(2,1)S(1)} %bitcast.112, bf16[1280,2560]{1,0:T(8,128)(2,1)} %param.17), kind=kOutput, calls=%fused_computation.100 | convolution fusion | flops 1677721600 | bytes 9830400 | tf_op jit(solution)/shard_map/dot_general | solution.py:129
  406.2 2.4 slice_bitcast_fusion
  408.6 30.9 %reduce-scatter.2.cloned.1.call-done = f32[64,2560]{1,0:T(8,128)} async-done(((f32[256,2560]{1,0:T(8,128)}), f32[64,2560]{1,0:T(8,128)}) %reduce-scatter.2.cloned.1.call-update) | async-done | bytes 655376 | tf_op jit(solution)/shard_map/reduce_scatter | solution.py:130
  (50 shorter events, 20.0 us)
Async XLA Ops:
  13.2 243.9 %all-to-all-start = ((bf16[128,1,16,2560]{3,2,1,0:T(8,128)(2,1)}), bf16[128,1,16,2560]{3,2,1,0:T(8,128)(2,1)}, u32[]{:S(2)}, u32[]{:S(2)}) async-start(bf16[128,1,16,2560]{3,2,1,0:T(8,128)(2,1)} %stack.2), calls=%async_computation | async-start | bytes 20971520 | tf_op jit(solution)/shard_map/all_to_all | solution.py:67
  30.0 299.5 %all-reduce.2.cloned.1.call-start = ((), (), s32[]{:S(2)}) async-start(), calls=%async_computation.2 | async-start | bytes 7864320 | tf_op jit(solution)/shard_map/psum | solution.py:86
  266.3 2.4 copy-start.1
  279.9 108.1 %all-gather.7.cloned.1.call-start = ((), (), s32[]{:S(2)}) async-start(), calls=%async_computation.4 | async-start | bytes 3932160 | tf_op jit(solution)/shard_map/all_gather | solution.py:12
  310.1 8.5 %copy-start.2 = (s32[1,4]{1,0:T(1,128)S(1)}, s32[1,4]{1,0:T(1,128)}, u32[]{:S(2)}) copy-start(s32[1,4]{1,0:T(1,128)} %param.14) | copy-start | bytes 52
  310.1 11.7 %copy-start.3 = (s32[1,256]{1,0:T(1,128)S(1)}, s32[1,256]{1,0:T(1,128)}, u32[]{:S(2)}) copy-start(s32[1,256]{1,0:T(1,128)} %param.13) | copy-start | bytes 3076
  334.8 1.7 slice-start
  344.4 14.5 %copy-start = (bf16[128,10,128]{2,0,1:T(8,128)(2,1)S(1)}, bf16[128,10,128]{2,0,1:T(8,128)(2,1)}, u32[]{:S(2)}) copy-start(bf16[128,10,128]{2,0,1:T(8,128)(2,1)} %copy.49) | copy-start | bytes 983044
  372.0 67.4 %reduce-scatter.2.cloned.1.call-start = ((), (), s32[]{:S(2)}) async-start(), calls=%async_computation.3 | async-start | bytes 3276800 | tf_op jit(solution)/shard_map/reduce_scatter | solution.py:130
Sparse Core Ops, SparseCore 0:
  280.0 35.6 all-reduce.1
  372.1 12.6 all-gather.6
  405.5 33.8 reduce-scatter.1
